TPU v7x, 32 devices: a whole 2x2x4 slice. The times are simulated.
32 devices in a mesh: seq: 8 (over z, y), chan: 4 (over x, core).
Axes of the slice: x: 2, y: 2, z: 4, core: 2. Of those that a mesh axis runs over, the one named last changes fastest.
Arguments:
- queries: bfloat16 [1024, 8192], P('seq', 'chan'), may hold values from -6 to 6
- key_in: bfloat16 [1024, 8192], P('seq', 'chan'), may hold values from -6 to 6
- values: bfloat16 [1024, 8192], P('seq', 'chan'), may hold values from -6 to 6
- decay_rates: float32 [8192], P('chan'), may hold values from 9.765625e-05 to 0.03
- skip_gain: float32 [8192], P('chan'), may hold values from -4 to 4
- out_gain: float32 [8192], P('chan'), may hold values from 0.5 to 1.5
- pos_weight: float32 [32, 64], replicated, may hold values from -1.5 to 1.5
- filt_weight: float32 [64, 8192], P(None, 'chan'), may hold values from -0.75 to 0.75
Outputs:
- layer_out: float32 [1024, 8192], P('seq', 'chan')
All inputs are finite; a program needn't handle non-finite values.
Results may differ from a plain program's by a relative error of at most 0.0075.
Values may be sent and summed in bfloat16 or wider, within the bound.
A program may use at most 128 MiB of HBM per device.

v0:
```python
import math

import jax
import jax.numpy as jnp
import numpy as np
from jax import lax
from jax.sharding import PartitionSpec as P

FREQS = 16


HIGHEST = lax.Precision.HIGHEST


def from_behind(block, axis, distance):
    devices = range(lax.axis_size(axis))
    route = [(i - distance, i) for i in devices if i - distance in devices]
    return lax.ppermute(block, axis, route)


def wave_table():
    return np.array([int(4096 * 2.0 ** (-e / 2.0)) for e in range(FREQS)], dtype=np.int32)


def features(position_grid):
    wave_numbers = jnp.asarray(wave_table())
    phases = position_grid[:, None] * wave_numbers[None, :] % 8192
    angles = phases.astype(jnp.float32) * (2.0 * math.pi / 8192.0)
    return jnp.concatenate([jnp.sin(angles), jnp.cos(angles)], axis=1)


def make_filter(position_grid, rate_factor, pos_weight, weight_part):
    hidden = jnp.tanh(jnp.dot(features(position_grid), pos_weight, precision=HIGHEST))
    filter_envelope = jnp.dot(hidden, weight_part, precision=HIGHEST)
    time_points = position_grid.astype(jnp.float32)[:, None]
    taps = (
        jnp.exp(-rate_factor[None, :] * time_points)
        * jnp.sqrt(2.0 * rate_factor)[None, :]
        * filter_envelope
    )
    return taps.astype(jnp.bfloat16)


def split_parts(operand):
    if operand.dtype == jnp.bfloat16:
        return [operand]
    upper = operand.astype(jnp.bfloat16)
    lower = (operand - upper.astype(jnp.float32)).astype(jnp.bfloat16)
    return [upper, lower]


def split_product(form, left, right):
    total = None
    for left_rank, left_part in enumerate(split_parts(left)):
        for right_rank, right_part in enumerate(split_parts(right)):
            if left_rank + right_rank < 2:
                term = jnp.einsum(form, left_part, right_part, preferred_element_type=jnp.float32)
                total = term if total is None else total + term
    return total


def split_length(length):
    outer_len = 1
    for divisor in range(1, math.isqrt(length) + 1):
        if length % divisor == 0:
            outer_len = divisor
    return (outer_len, length // outer_len)


def dft_tables(length):
    index_vector = jnp.arange(length, dtype=jnp.int32)
    angles = (index_vector[:, None] * index_vector[None, :] % length).astype(jnp.float32) * (
        2.0 * math.pi / length
    )
    return (jnp.cos(angles), jnp.sin(angles))


def twiddles(outer_len, inner_len):
    length = outer_len * inner_len
    products = (
        jnp.arange(outer_len, dtype=jnp.int32)[:, None]
        * jnp.arange(inner_len, dtype=jnp.int32)[None, :]
        % length
    )
    angles = products.astype(jnp.float32) * (2.0 * math.pi / length)
    return (jnp.cos(angles)[:, :, None], jnp.sin(angles)[:, :, None])


def forward(signal, outer_len, inner_len):
    grid_in = signal.reshape(outer_len, inner_len, signal.shape[1])
    cos_outer, sin_outer = dft_tables(outer_len)
    cos_inner, sin_inner = dft_tables(inner_len)
    twid_cos, twid_sin = twiddles(outer_len, inner_len)
    section_re = split_product("kn,nmc->kmc", cos_outer, grid_in)
    section_im = -split_product("kn,nmc->kmc", sin_outer, grid_in)
    turned_re = section_re * twid_cos + section_im * twid_sin
    turned_im = section_im * twid_cos - section_re * twid_sin
    real_part = split_product("kmc,jm->kjc", turned_re, cos_inner) + split_product(
        "kmc,jm->kjc", turned_im, sin_inner
    )
    imag_part = split_product("kmc,jm->kjc", turned_im, cos_inner) - split_product(
        "kmc,jm->kjc", turned_re, sin_inner
    )
    return (real_part, imag_part)


def inverse_result(real_part, imag_part, outer_len, inner_len):
    cos_outer, sin_outer = dft_tables(outer_len)
    cos_inner, sin_inner = dft_tables(inner_len)
    twid_cos, twid_sin = twiddles(outer_len, inner_len)
    section_re = split_product("kjc,mj->kmc", real_part, cos_inner) - split_product(
        "kjc,mj->kmc", imag_part, sin_inner
    )
    section_im = split_product("kjc,mj->kmc", imag_part, cos_inner) + split_product(
        "kjc,mj->kmc", real_part, sin_inner
    )
    turned_re = section_re * twid_cos - section_im * twid_sin
    turned_im = section_im * twid_cos + section_re * twid_sin
    signal = split_product("kn,kmc->nmc", cos_outer, turned_re) - split_product(
        "kn,kmc->nmc", sin_outer, turned_im
    )
    return signal.reshape(outer_len * inner_len, real_part.shape[2]) / (outer_len * inner_len)


def local(queries, key_in, values, decay_rates, skip_gain, out_gain, pos_weight, filt_weight):
    tok_rows, chan_cols = queries.shape
    seq_count = lax.axis_size("seq")
    mixed_kv = (key_in.astype(jnp.float32) * values.astype(jnp.float32)).astype(jnp.bfloat16)
    outer_len, inner_len = split_length(2 * tok_rows)
    blank_rows = jnp.zeros((tok_rows, chan_cols), jnp.bfloat16)

    def cycle_step(lag_index, state_in):
        carried, preceding_values, accum_re, accum_im = state_in
        lag_pos = lag_index * tok_rows + jnp.arange(tok_rows, dtype=jnp.int32)
        segment_new = make_filter(lag_pos, decay_rates, pos_weight, filt_weight)
        filt_re, filt_im = forward(
            jnp.concatenate([preceding_values, segment_new], axis=0), outer_len, inner_len
        )
        data_re, data_im = forward(
            jnp.concatenate([carried, blank_rows], axis=0), outer_len, inner_len
        )
        accum_re = accum_re + filt_re * data_re - filt_im * data_im
        accum_im = accum_im + filt_re * data_im + filt_im * data_re
        carried = from_behind(carried, "seq", 1)
        return (carried, segment_new, accum_re, accum_im)

    empty_spec = jnp.zeros((outer_len, inner_len, chan_cols), jnp.float32)
    start_state = (mixed_kv, blank_rows, empty_spec, empty_spec)
    final_state = lax.fori_loop(0, seq_count, cycle_step, start_state)
    long_conv = inverse_result(final_state[2], final_state[3], outer_len, inner_len)[tok_rows:]
    gated = queries.astype(jnp.float32) * (
        long_conv + skip_gain[None, :] * mixed_kv.astype(jnp.float32)
    )
    row_sums = lax.psum(jnp.sum(gated * gated, axis=1), "chan")
    inv_rms = lax.rsqrt(row_sums / (chan_cols * lax.axis_size("chan")) + 1e-06)
    return gated * inv_rms[:, None] * out_gain[None, :]


def solution(mesh):
    in_specs = (
        P("seq", "chan"),
        P("seq", "chan"),
        P("seq", "chan"),
        P("chan"),
        P("chan"),
        P("chan"),
        P(),
        P(None, "chan"),
    )
    out_specs = P("seq", "chan")
    return jax.shard_map(local, mesh=mesh, in_specs=in_specs, out_specs=out_specs, check_vma=False)
```

profile of v0, /device:TPU:0, one launch (start us, length us, event | category | flops | bytes accessed | tf_op | source)
XLA Modules:
  0.0 685.9 jit_solution(6778479636527356985)
XLA Ops:
  3.0 649.6 %while.24 = (s32[]{:T(128)}, bf16[128,2048]{1,0:T(8,128)(2,1)}, bf16[128,2048]{1,0:T(8,128)(2,1)S(1)}, f32[16,16,2048]{2,1,0:T(8,128)S(1)}, f32[16,16,2048]{2,1,...) while((s32[]{:T(128)}, bf16[128,2048]{1,0:T(8,128)(2,1)}, ...), condition=%wide.region_1.2_spmd.clone.clone, body=%wide.region_0.1_spmd.sunk.clone.clone.sunk | while | flops 778480000 | bytes 283790080 | solution.py:149
  5.3 5.7 collective-permute-start
  28.7 6.7 subtract_convert_fusion.17
  48.3 2.8 convolution_add_fusion.50
  59.3 2.8 convolution_add_fusion.45
  62.0 2.8 convolution_add_fusion.44
  67.6 3.1 convolution_add_fusion.52
  87.6 3.5 collective-permute-start
  108.8 6.4 subtract_convert_fusion.17
  128.2 2.9 convolution_add_fusion.50
  147.5 3.1 convolution_add_fusion.52
  167.5 3.5 collective-permute-start
  188.6 6.7 subtract_convert_fusion.17
  208.3 2.8 convolution_add_fusion.50
  219.2 2.8 convolution_add_fusion.45
  222.0 2.8 convolution_add_fusion.44
  227.6 3.1 convolution_add_fusion.52
  247.6 3.5 collective-permute-start
  268.8 6.4 subtract_convert_fusion.17
  288.2 2.9 convolution_add_fusion.50
  299.2 2.8 convolution_add_fusion.45
  302.0 2.8 convolution_add_fusion.44
  307.5 3.1 convolution_add_fusion.52
  327.5 3.5 collective-permute-start
  348.6 6.7 subtract_convert_fusion.17
  368.3 2.8 convolution_add_fusion.50
  379.2 2.8 convolution_add_fusion.45
  382.0 2.8 convolution_add_fusion.44
  387.5 3.1 convolution_add_fusion.52
  407.6 3.5 collective-permute-start
  428.8 6.4 subtract_convert_fusion.17
  448.2 2.9 convolution_add_fusion.50
  459.2 2.8 convolution_add_fusion.45
  462.0 2.8 convolution_add_fusion.44
  467.5 3.1 convolution_add_fusion.52
  487.5 3.4 collective-permute-start
  508.6 6.7 subtract_convert_fusion.17
  528.3 2.8 convolution_add_fusion.50
  539.2 2.8 convolution_add_fusion.45
  542.0 2.8 convolution_add_fusion.44
  547.5 3.1 convolution_add_fusion.52
  587.4 6.4 subtract_convert_fusion.17
  606.8 2.9 convolution_add_fusion.50
  617.8 2.8 convolution_add_fusion.45
  620.6 2.8 convolution_add_fusion.44
  626.1 3.1 convolution_add_fusion.52
  664.6 4.0 subtract_convert_fusion.7
  678.7 5.7 psum.7
  (649 shorter events, 498.1 us)
Async XLA Ops:
  0.0 3.0 copy-start.23
  0.0 3.0 copy-start.21
  0.0 3.0 copy-start.20
  0.0 3.0 copy-start.25
  5.3 78.7 %collective-permute-start = (bf16[128,2048]{1,0:T(8,128)(2,1)}, bf16[128,2048]{1,0:T(8,128)(2,1)}, u32[]{:S(2)}, u32[]{:S(2)}) collective-permute-start(bf16[128,2048]{1,0:T(8,128)(2,1)} %copy.348), channel_id=1, source_target_pairs={{0,4},{4,8},{8,12},{12,16},{16,20},{20,24},{24,28},{1,5},{5,9},{9,... | collective-permute-start | bytes 1572872 | tf_op jit(solution)/shard_map/while/body/eval_jaxpr/ppermute | solution.py:18
  64.8 2.7 copy-start.6
  67.6 3.1 copy-start.5
  67.6 3.1 copy-start.12
  81.5 3.9 copy-start.16
  81.5 3.9 copy-start.26
  87.6 76.5 %collective-permute-start = (bf16[128,2048]{1,0:T(8,128)(2,1)}, bf16[128,2048]{1,0:T(8,128)(2,1)}, u32[]{:S(2)}, u32[]{:S(2)}) collective-permute-start(bf16[128,2048]{1,0:T(8,128)(2,1)} %copy.348), channel_id=1, source_target_pairs={{0,4},{4,8},{8,12},{12,16},{16,20},{20,24},{24,28},{1,5},{5,9},{9,... | collective-permute-start | bytes 1572872 | tf_op jit(solution)/shard_map/while/body/eval_jaxpr/ppermute | solution.py:18
  147.5 3.1 copy-start.5
  147.5 3.1 copy-start.12
  161.6 3.9 copy-start.16
  161.6 3.9 copy-start.26
  167.5 76.5 %collective-permute-start = (bf16[128,2048]{1,0:T(8,128)(2,1)}, bf16[128,2048]{1,0:T(8,128)(2,1)}, u32[]{:S(2)}, u32[]{:S(2)}) collective-permute-start(bf16[128,2048]{1,0:T(8,128)(2,1)} %copy.348), channel_id=1, source_target_pairs={{0,4},{4,8},{8,12},{12,16},{16,20},{20,24},{24,28},{1,5},{5,9},{9,... | collective-permute-start | bytes 1572872 | tf_op jit(solution)/shard_map/while/body/eval_jaxpr/ppermute | solution.py:18
  227.6 3.1 copy-start.5
  227.6 3.1 copy-start.12
  241.5 3.9 copy-start.16
  241.5 3.9 copy-start.26
  247.6 76.5 %collective-permute-start = (bf16[128,2048]{1,0:T(8,128)(2,1)}, bf16[128,2048]{1,0:T(8,128)(2,1)}, u32[]{:S(2)}, u32[]{:S(2)}) collective-permute-start(bf16[128,2048]{1,0:T(8,128)(2,1)} %copy.348), channel_id=1, source_target_pairs={{0,4},{4,8},{8,12},{12,16},{16,20},{20,24},{24,28},{1,5},{5,9},{9,... | collective-permute-start | bytes 1572872 | tf_op jit(solution)/shard_map/while/body/eval_jaxpr/ppermute | solution.py:18
  304.8 2.7 copy-start.6
  307.5 3.1 copy-start.5
  307.5 3.1 copy-start.12
  321.6 3.9 copy-start.16
  321.6 3.9 copy-start.26
  327.5 76.5 %collective-permute-start = (bf16[128,2048]{1,0:T(8,128)(2,1)}, bf16[128,2048]{1,0:T(8,128)(2,1)}, u32[]{:S(2)}, u32[]{:S(2)}) collective-permute-start(bf16[128,2048]{1,0:T(8,128)(2,1)} %copy.348), channel_id=1, source_target_pairs={{0,4},{4,8},{8,12},{12,16},{16,20},{20,24},{24,28},{1,5},{5,9},{9,... | collective-permute-start | bytes 1572872 | tf_op jit(solution)/shard_map/while/body/eval_jaxpr/ppermute | solution.py:18
  387.5 3.1 copy-start.5
  387.5 3.1 copy-start.12
  401.5 3.9 copy-start.16
  401.5 3.9 copy-start.26
  407.6 76.5 %collective-permute-start = (bf16[128,2048]{1,0:T(8,128)(2,1)}, bf16[128,2048]{1,0:T(8,128)(2,1)}, u32[]{:S(2)}, u32[]{:S(2)}) collective-permute-start(bf16[128,2048]{1,0:T(8,128)(2,1)} %copy.348), channel_id=1, source_target_pairs={{0,4},{4,8},{8,12},{12,16},{16,20},{20,24},{24,28},{1,5},{5,9},{9,... | collective-permute-start | bytes 1572872 | tf_op jit(solution)/shard_map/while/body/eval_jaxpr/ppermute | solution.py:18
  464.8 2.7 copy-start.6
  467.5 3.1 copy-start.5
  467.5 3.1 copy-start.12
  481.5 3.9 copy-start.16
  481.5 3.9 copy-start.26
  487.5 76.5 %collective-permute-start = (bf16[128,2048]{1,0:T(8,128)(2,1)}, bf16[128,2048]{1,0:T(8,128)(2,1)}, u32[]{:S(2)}, u32[]{:S(2)}) collective-permute-start(bf16[128,2048]{1,0:T(8,128)(2,1)} %copy.348), channel_id=1, source_target_pairs={{0,4},{4,8},{8,12},{12,16},{16,20},{20,24},{24,28},{1,5},{5,9},{9,... | collective-permute-start | bytes 1572872 | tf_op jit(solution)/shard_map/while/body/eval_jaxpr/ppermute | solution.py:18
  547.5 3.1 copy-start.5
  547.5 3.1 copy-start.12
  561.4 3.9 copy-start.16
  561.4 3.9 copy-start.26
  567.6 75.1 %collective-permute-start = (bf16[128,2048]{1,0:T(8,128)(2,1)}, bf16[128,2048]{1,0:T(8,128)(2,1)}, u32[]{:S(2)}, u32[]{:S(2)}) collective-permute-start(bf16[128,2048]{1,0:T(8,128)(2,1)} %copy.348), channel_id=1, source_target_pairs={{0,4},{4,8},{8,12},{12,16},{16,20},{20,24},{24,28},{1,5},{5,9},{9,... | collective-permute-start | bytes 1572872 | tf_op jit(solution)/shard_map/while/body/eval_jaxpr/ppermute | solution.py:18
  626.1 3.1 copy-start.5
  626.1 3.1 copy-start.12
  640.1 3.9 copy-start.16
  640.2 3.9 copy-start.26
  677.2 7.2 %copy-start.24 = (f32[2048]{0:T(1024)S(1)}, f32[2048]{0:T(1024)}, u32[]{:S(2)}) copy-start(f32[2048]{0:T(1024)} %param.16) | copy-start | bytes 24580
  (99 other events, 166.3 us)
where the time goes:
time: 689 us; the launch traced here: 686 us
  matrix products  574 us (83%)
  local copies, waits for them, and re-layouts  57.8 us (8%)
  starting transfers between devices  28.5 us (4%)
  loops' own time  12.6 us (2%)
    dot_general x274, matrix products, split_product(): jnp.einsum(form, left_part, right_part, preferred_element_type=jnp.float32)  563 us
    while x264, local copies, waits for them, and re-layouts  44.6 us
    ppermute x8, starting transfers between devices, from_behind(): return lax.ppermute(block, axis, route)  28.5 us
  transfers between devices with their start and end apart: 8, of which 0 were waited for; matrix products, arithmetic and copies ran while one was open for 82% of the time, Pallas kernels for 0%

commit v1 on v0

v1 whole, which is shorter than its diff:
```python
import functools
import math

import jax
import jax.numpy as jnp
import numpy as np
from jax import lax
from jax.experimental import pallas as pl
from jax.experimental.pallas import tpu as pltpu
from jax.sharding import PartitionSpec as P

FREQS = 16
LANES = 128
HIGHEST = lax.Precision.HIGHEST
MESH = pl.DeviceIdType.MESH


def feature_table(length):
    waves = np.array([int(4096 * 2.0 ** (-e / 2.0)) for e in range(FREQS)], dtype=np.int64)
    phases = np.arange(length, dtype=np.int64)[:, None] * waves[None, :] % 8192
    angles = phases * (2.0 * math.pi / 8192.0)
    return np.concatenate([np.sin(angles), np.cos(angles)], axis=1).astype(np.float32)


def spectral_tables(length, block):
    k = np.arange(length, dtype=np.int64)
    turns = (2 * k[:, None] + 1) * k[None, :] % (4 * length)
    angles = turns * (math.pi / (2 * length))
    both = np.stack([np.cos(angles), np.sin(angles)]).reshape(2, length // block, block, length)
    forward = both.transpose(1, 0, 2, 3).reshape(2 * length, length)
    backward = forward.T / length
    return forward.astype(jnp.bfloat16), backward.astype(jnp.bfloat16)


def plain(queries, key_in, values, decay_rates, skip_gain, out_gain, pos_weight, filt_weight):
    rows, cols = queries.shape
    seq_count = lax.axis_size("seq")
    length, width = rows * seq_count, cols // seq_count
    forward, backward = (jnp.asarray(t) for t in spectral_tables(length, length))
    mixed = (key_in.astype(jnp.float32) * values.astype(jnp.float32)).astype(jnp.bfloat16)
    data = lax.all_to_all(mixed, "seq", 1, 0, tiled=True)
    start = lax.axis_index("seq") * width
    rates = lax.dynamic_slice_in_dim(decay_rates, start, width)
    weights = lax.dynamic_slice_in_dim(filt_weight, start, width, 1)
    hidden = jnp.tanh(jnp.dot(jnp.asarray(feature_table(length)), pos_weight, precision=HIGHEST))
    profile = jnp.dot(hidden, weights, precision=HIGHEST)
    time = jnp.arange(length, dtype=jnp.float32)[:, None]
    taps = (jnp.exp(-rates[None, :] * time) * jnp.sqrt(2.0 * rates)[None, :] * profile).astype(jnp.bfloat16)
    filt_spec = jnp.dot(forward, taps, preferred_element_type=jnp.float32)
    data_spec = jnp.dot(forward, data, preferred_element_type=jnp.float32)
    fc, fs, dc, ds = filt_spec[:length], filt_spec[length:], data_spec[:length], data_spec[length:]
    spec = jnp.concatenate([fc * dc - fs * ds, fc * ds + fs * dc], axis=0).astype(jnp.bfloat16)
    conv = jnp.dot(backward, spec, preferred_element_type=jnp.float32).astype(jnp.bfloat16)
    conv = lax.all_to_all(conv, "seq", 0, 1, tiled=True).astype(jnp.float32)
    gated = queries.astype(jnp.float32) * (conv + skip_gain[None, :] * mixed.astype(jnp.float32))
    row_sums = lax.psum(jnp.sum(gated * gated, axis=1), "chan")
    inv_rms = lax.rsqrt(row_sums / (cols * lax.axis_size("chan")) + 1e-06)
    return gated * inv_rms[:, None] * out_gain[None, :]


def solution(mesh):
    in_specs = (
        P("seq", "chan"),
        P("seq", "chan"),
        P("seq", "chan"),
        P("chan"),
        P("chan"),
        P("chan"),
        P(),
        P(None, "chan"),
    )
    return jax.shard_map(
        plain, mesh=mesh, in_specs=in_specs, out_specs=P("seq", "chan"), check_vma=False
    )
```

time: 689 us -> 60 us (0.09)
  matrix products: 574 us -> 12.4 us
  local copies, waits for them, and re-layouts: 57.8 us -> 6.82 us
  waiting for transfers between devices: 0.02 us -> 21.5 us
  starting transfers between devices: 28.5 us -> 11.1 us
  loops' own time: 12.6 us -> 0 us
    dot_general x290 -> x6, matrix products: 574 us -> 12.4 us  [the longest x1 4.79 us: plain(): filt_spec = jnp.dot(forward, taps, preferred_element_type=jnp.float32)]
    while x264 -> x0, local copies, waits for them, and re-layouts: 44.6 us -> none
    ppermute x8 -> x0, starting transfers between devices: 28.5 us -> none  [from_behind(): return lax.ppermute(block, axis, route)]
    all_to_all x0 -> x2, waiting for transfers between devices: none -> 21.5 us  [the longest x1 14.4 us: plain(): conv = lax.all_to_all(conv, 'seq', 0, 1, tiled=True).astype(jnp.float32)]
    another operation x1 -> x0, loops' own time: 12.6 us -> none  [local(): final_state = lax.fori_loop(0, seq_count, cycle_step, start_state)]
    all_to_all x0 -> x2, starting transfers between devices: none -> 11.1 us  [the longest x1 7.28 us: plain(): data = lax.all_to_all(mixed, 'seq', 1, 0, tiled=True)]
    concatenate x8 -> x0, local copies, waits for them, and re-layouts: 9.2 us -> none  [cycle_step(): jnp.concatenate([carried, blank_rows], axis=0)]
  transfers between devices with their start and end apart: 8 -> 2, of which waited for: 0 -> 2; matrix products, arithmetic and copies ran while one was open for 82% -> 13% of each run, Pallas kernels for 0% -> 0%
where the time goes in v1:
time: 60 us; the launch traced here: 59.5 us
  waiting for transfers between devices  21.5 us (36%)
  matrix products  12.4 us (21%)
  starting transfers between devices  11.1 us (18%)
  local copies, waits for them, and re-layouts  6.82 us (11%)
  blocking collectives  5.66 us (9%)
  other arithmetic  1.97 us (3%)
    all_to_all x1, waiting for transfers between devices, plain(): conv = lax.all_to_all(conv, 'seq', 0, 1, tiled=True).astype(jnp.float32)  14.4 us
    all_to_all x1, starting transfers between devices, plain(): data = lax.all_to_all(mixed, 'seq', 1, 0, tiled=True)  7.28 us
    all_to_all x1, waiting for transfers between devices, plain(): data = lax.all_to_all(mixed, 'seq', 1, 0, tiled=True)  7.11 us
    psum x1, blocking collectives, plain(): row_sums = lax.psum(jnp.sum(gated * gated, axis=1), 'chan')  5.66 us
    dot_general x1, matrix products, plain(): filt_spec = jnp.dot(forward, taps, preferred_element_type=jnp.float32)  4.79 us
    dot_general x1, matrix products, plain(): data_spec = jnp.dot(forward, data, preferred_element_type=jnp.float32)  3.86 us
    all_to_all x1, starting transfers between devices, plain(): conv = lax.all_to_all(conv, 'seq', 0, 1, tiled=True).astype(jnp.float32)  3.77 us
    unnamed x21, local copies, waits for them, and re-layouts  3.61 us
  transfers between devices with their start and end apart: 2, of which 2 were waited for; matrix products, arithmetic and copies ran while one was open for 13% of the time, Pallas kernels for 0%

profile of v1, /device:TPU:0, one launch (start us, length us, event | category | flops | bytes accessed | tf_op | source)
XLA Modules:
  0.0 59.5 jit_solution(1241027660104808712)
XLA Ops:
  0.0 0.0 copy-start
  0.0 1.4 %copy.16 = bf16[128,2048]{0,1:T(8,128)(2,1)S(1)} copy(bf16[128,2048]{1,0:T(8,128)(2,1)} %param.12) | data formatting | bytes 1048576 | tf_op args[1]
  1.4 1.3 %copy.17 = bf16[128,2048]{0,1:T(8,128)(2,1)S(1)} copy(bf16[128,2048]{1,0:T(8,128)(2,1)} %param.13) | data formatting | bytes 1048576 | tf_op args[2]
  2.7 0.0 copy-start.5
  2.7 0.0 copy-start.7
  2.7 0.1 multiply_convert_fusion
  2.9 1.0 %copy.18 = bf16[128,8,256]{2,0,1:T(8,128)(2,1)} copy(bf16[128,8,256]{0,2,1:T(8,128)(2,1)S(1)} %bitcast.28) | data formatting | bytes 1048576 | tf_op jit(solution)/shard_map/all_to_all | solution.py:41
  3.9 7.3 %all-to-all-start = ((bf16[128,8,256]{2,0,1:T(8,128)(2,1)}), bf16[128,8,256]{2,0,1:T(8,128)(2,1)}, u32[]{:S(2)}, u32[]{:S(2)}) async-start(bf16[128,8,256]{2,0,1:T(8,128)(2,1)} %copy.18), calls=%async_computation | async-start | bytes 1048576 | tf_op jit(solution)/shard_map/all_to_all | solution.py:41
  11.2 0.8 %dynamic-slice_negate_fusion = (f32[256]{0:T(256)S(1)}, f32[256]{0:T(256)S(1)}) fusion(f32[2048]{0:T(1024)} %param.14, s32[]{:T(128)S(6)} %select_n.4), kind=kLoop, calls=%fused_computation.19 | loop fusion | flops 512 | bytes 3076 | tf_op jit(solution)/shard_map/neg | solution.py:48
  11.9 0.0 copy-done.5
  11.9 0.0 copy-done.7
  11.9 0.7 %convolution_tanh_fusion = f32[1024,64]{0,1:T(8,128)S(1)} fusion(f32[1024,32]{1,0:T(8,128)S(1)} %copy-done.5, f32[32,64]{1,0:T(8,128)S(1)} %copy-done.7), kind=kOutput, calls=%fused_computation.5 | convolution fusion | flops 25165824 | bytes 401408 | tf_op jit(solution)/shard_map/dot_general | solution.py:45
  12.7 0.0 copy-done
  12.7 1.2 %fusion = bf16[1024,256]{1,0:T(8,128)(2,1)S(1)} fusion(f32[1024,64]{0,1:T(8,128)S(1)} %convolution_tanh_fusion, f32[256]{0:T(256)S(1)} %get-tuple-element.6, f32[256]{0:T(256)S(1)} %get-tuple-element.5, f32[64,2048]{1,0:T(8,128)S(1)} %copy-done, s32[]{:T(128)S(6)} %select_n.4), kind=kOutput, calls=%fused_computation.2 | convolution fusion | flops 202375168 | bytes 854020 | tf_op jit(solution)/shard_map/dot_general | solution.py:46
  13.8 4.8 %fusion.8 = f32[2048,256]{1,0:T(8,128)} fusion(bf16[2048,1024]{1,0:T(8,128)(2,1)} %constant.27.clone, bf16[1024,256]{1,0:T(8,128)(2,1)S(1)} %fusion), kind=kOutput, calls=%fused_computation.22 | convolution fusion | flops 1073741824 | bytes 6815744 | tf_op jit(solution)/shard_map/dot_general | solution.py:49
  18.6 0.0 copy-start.1
  18.6 7.1 %all-to-all-done = bf16[128,8,256]{2,0,1:T(8,128)(2,1)} async-done(((bf16[128,8,256]{2,0,1:T(8,128)(2,1)}), bf16[128,8,256]{2,0,1:T(8,128)(2,1)}, u32[]{:S(2)}, u32[]{:S(2)}) %all-to-all-start) | async-done | bytes 524320 | tf_op jit(solution)/shard_map/all_to_all | solution.py:41
  25.8 0.0 copy-start.2
  25.8 3.9 %fusion.4 = f32[2048,256]{1,0:T(8,128)S(1)} fusion(bf16[2048,1024]{1,0:T(8,128)(2,1)} %constant.32, bf16[128,8,256]{2,0,1:T(8,128)(2,1)} %all-to-all-done), kind=kOutput, calls=%fused_computation.15 | convolution fusion | flops 1073741824 | bytes 6815744 | tf_op jit(solution)/shard_map/dot_general | solution.py:50
  29.6 0.0 copy-done.1
  29.6 0.0 copy-done.2
  29.6 0.0 copy-start.3
  29.7 1.0 %fusion.5 = f32[256,1024]{1,0:T(8,128)S(1)} fusion(bf16[1024,1024]{1,0:T(8,128)(2,1)S(1)} %copy-done.1, f32[2048,256]{1,0:T(8,128)S(1)} %fusion.4, f32[2048,256]{1,0:T(8,128)S(1)} %copy-done.2), kind=kOutput, calls=%fused_computation.16 | convolution fusion | flops 537919488 | bytes 7340032 | tf_op jit(solution)/shard_map/dot_general | solution.py:53
  30.6 0.6 %copy-done.3 = bf16[1024,1024]{1,0:T(8,128)(2,1)S(1)} copy-done((bf16[1024,1024]{1,0:T(8,128)(2,1)S(1)}, bf16[1024,1024]{1,0:T(8,128)(2,1)}, u32[]{:S(2)}) %copy-start.3) | copy-done | bytes 2097176
  31.2 0.9 %fusion.2 = bf16[32,8,8,128]{3,2,1,0:T(8,128)(2,1)S(1)} fusion(f32[256,1024]{1,0:T(8,128)S(1)} %fusion.5, bf16[1024,1024]{1,0:T(8,128)(2,1)S(1)} %copy-done.3, f32[2048,256]{1,0:T(8,128)S(1)} %fusion.4, f32[2048,256]{1,0:T(8,128)S(1)} %copy-done.2), kind=kOutput, calls=%fused_computation.4 | convolution fusion | flops 538443776 | bytes 7864320 | tf_op jit(solution)/shard_map/dot_general | solution.py:53
  32.1 0.0 copy-start.4
  32.1 0.0 copy-start.6
  32.1 0.9 %copy.26 = bf16[32,8,8,128]{3,2,0,1:T(8,128)(2,1)} copy(bf16[32,8,8,128]{3,2,1,0:T(8,128)(2,1)S(1)} %fusion.2) | data formatting | bytes 1048576 | tf_op jit(solution)/shard_map/all_to_all | solution.py:54
  33.0 0.0 copy-start.8
  33.0 3.8 %all-to-all-start.1 = ((bf16[8,128,256]{1,2,0:T(8,128)(2,1)}), bf16[8,128,256]{1,2,0:T(8,128)(2,1)S(1)}, u32[]{:S(2)}, u32[]{:S(2)}) async-start(bf16[8,128,256]{1,2,0:T(8,128)(2,1)} %bitcast.27), calls=%async_computation.1 | async-start | bytes 1048576 | tf_op jit(solution)/shard_map/all_to_all | solution.py:54
  36.8 0.0 copy-done.4
  36.8 0.3 copy.15
  37.1 14.4 %all-to-all-done.1 = bf16[8,128,256]{1,2,0:T(8,128)(2,1)S(1)} async-done(((bf16[8,128,256]{1,2,0:T(8,128)(2,1)}), bf16[8,128,256]{1,2,0:T(8,128)(2,1)S(1)}, u32[]{:S(2)}, u32[]{:S(2)}) %all-to-all-start.1) | async-done | bytes 524320 | tf_op jit(solution)/shard_map/all_to_all | solution.py:54
  51.5 0.0 copy-done.6
  51.5 0.4 multiply_reduce_fusion
  51.8 5.7 %psum.7 = f32[128]{0:T(128)S(1)} all-reduce(f32[128]{0:T(128)S(1)} %multiply_reduce_fusion), channel_id=1, replica_groups=mesh['seq'=8,'chan'=4] {'chan'}, use_global_device_ids=true, to_apply=%region_1.0 | all-reduce | flops 128 | bytes 1024 | tf_op jit(solution)/shard_map/psum | solution.py:56
  57.5 0.0 copy-done.8
  57.5 0.7 %multiply_multiply_fusion = f32[128,2048]{0,1:T(8,128)S(1)} fusion(f32[2048]{0:T(1024)S(1)} %copy-done.8, f32[128]{0:T(128)S(1)} %add_rsqrt_fusion, bf16[128,2048]{0,1:T(8,128)(2,1)S(1)} %multiply_convert_fusion, f32[2048]{0:T(1024)S(1)} %copy-done.6, bf16[128,2048]{0,1:T(8,128)(2,1)S(1)} %copy.15, bf16[8,128,256]{1,2,0:T(8,128)(2,1)S(1)} %all-to-all-done.1), kind=kLoop, calls=%fused_computation.8 | loop fusion | flops 2097152 | bytes 2638336 | tf_op jit(solution)/shard_map/mul | solution.py:58
  58.2 1.3 %copy.21 = f32[128,2048]{1,0:T(8,128)} copy(f32[128,2048]{0,1:T(8,128)S(1)} %multiply_multiply_fusion) | data formatting | bytes 2097152 | tf_op jit(solution)/shard_map/mul | solution.py:58
  (1 shorter events, 0.0 us)
Async XLA Ops:
  0.0 12.7 %copy-start = (f32[64,2048]{1,0:T(8,128)S(1)}, f32[64,2048]{1,0:T(8,128)}, u32[]{:S(2)}) copy-start(f32[64,2048]{1,0:T(8,128)} %param.18) | copy-start | bytes 1572868
  2.7 9.2 %copy-start.5 = (f32[1024,32]{1,0:T(8,128)S(1)}, f32[1024,32]{1,0:T(8,128)}, u32[]{:S(2)}) copy-start(f32[1024,32]{1,0:T(8,128)} %constant.29.clone) | copy-start | bytes 393220
  2.7 9.2 %copy-start.7 = (f32[32,64]{1,0:T(8,128)S(1)}, f32[32,64]{1,0:T(8,128)}, u32[]{:S(2)}) copy-start(f32[32,64]{1,0:T(8,128)} %param.17) | copy-start | bytes 24580
  3.9 21.9 %all-to-all-start = ((bf16[128,8,256]{2,0,1:T(8,128)(2,1)}), bf16[128,8,256]{2,0,1:T(8,128)(2,1)}, u32[]{:S(2)}, u32[]{:S(2)}) async-start(bf16[128,8,256]{2,0,1:T(8,128)(2,1)} %copy.18), calls=%async_computation | async-start | bytes 1048576 | tf_op jit(solution)/shard_map/all_to_all | solution.py:41
  18.6 11.0 %copy-start.1 = (bf16[1024,1024]{1,0:T(8,128)(2,1)S(1)}, bf16[1024,1024]{1,0:T(8,128)(2,1)}, u32[]{:S(2)}) copy-start(bf16[1024,1024]{1,0:T(8,128)(2,1)} %constant.33) | copy-start | bytes 6291460
  25.8 3.9 %copy-start.2 = (f32[2048,256]{1,0:T(8,128)S(1)}, f32[2048,256]{1,0:T(8,128)}, u32[]{:S(2)}) copy-start(f32[2048,256]{1,0:T(8,128)} %fusion.8) | copy-start | bytes 6291460
  29.6 1.6 %copy-start.3 = (bf16[1024,1024]{1,0:T(8,128)(2,1)S(1)}, bf16[1024,1024]{1,0:T(8,128)(2,1)}, u32[]{:S(2)}) copy-start(bf16[1024,1024]{1,0:T(8,128)(2,1)} %constant.34) | copy-start | bytes 6291460
  32.1 4.7 %copy-start.4 = (bf16[128,2048]{1,0:T(8,128)(2,1)S(1)}, bf16[128,2048]{1,0:T(8,128)(2,1)}, u32[]{:S(2)}) copy-start(bf16[128,2048]{1,0:T(8,128)(2,1)} %param.11) | copy-start | bytes 1572868
  32.1 19.3 %copy-start.6 = (f32[2048]{0:T(1024)S(1)}, f32[2048]{0:T(1024)}, u32[]{:S(2)}) copy-start(f32[2048]{0:T(1024)} %param.15) | copy-start | bytes 24580
  33.0 24.5 %copy-start.8 = (f32[2048]{0:T(1024)S(1)}, f32[2048]{0:T(1024)}, u32[]{:S(2)}) copy-start(f32[2048]{0:T(1024)} %param.16) | copy-start | bytes 24580
  33.0 18.4 %all-to-all-start.1 = ((bf16[8,128,256]{1,2,0:T(8,128)(2,1)}), bf16[8,128,256]{1,2,0:T(8,128)(2,1)S(1)}, u32[]{:S(2)}, u32[]{:S(2)}) async-start(bf16[8,128,256]{1,2,0:T(8,128)(2,1)} %bitcast.27), calls=%async_computation.1 | async-start | bytes 1048576 | tf_op jit(solution)/shard_map/all_to_all | solution.py:54

commit v2 on v1

--- a/solution.py
+++ b/solution.py
@@ -58,6 +58,236 @@
     return gated * inv_rms[:, None] * out_gain[None, :]
 
 
+def kernel(
+    n, m, block,
+    q_hbm, k_hbm, v_hbm, rates_ref, skip_ref, feats_ref, pos_ref, weight_hbm, fwd_hbm, bwd_hbm,
+    gated_ref, inv_ref,
+    q_buf, k_buf, v_buf, weight_buf, fwd_buf, bwd_buf,
+    mixed, data, taps, filt_spec, spec, conv, back, sums_out, sums_in,
+    in_sem, send1, recv1, send2, recv2, send3, recv3,
+):
+    rows, cols = q_buf.shape
+    length, width = taps.shape
+    chunks = width // LANES
+    me, lane = lax.axis_index("seq"), lax.axis_index("chan")
+    order = sorted(range(1, n), key=lambda k: abs(k - n // 2))
+
+    def seq_peer(k):
+        return lax.rem(me + k, n)
+
+    barrier = pltpu.get_barrier_semaphore()
+    for k in range(1, n):
+        pl.semaphore_signal(barrier, inc=1, device_id=(seq_peer(k), lane), device_id_type=MESH)
+    for k in range(1, m):
+        pl.semaphore_signal(barrier, inc=1, device_id=(me, lax.rem(lane + k, m)), device_id_type=MESH)
+
+    own = pl.ds(pl.multiple_of(me * width, LANES), width)
+    loads = [
+        pltpu.make_async_copy(k_hbm, k_buf, in_sem.at[0]),
+        pltpu.make_async_copy(v_hbm, v_buf, in_sem.at[1]),
+        pltpu.make_async_copy(weight_hbm.at[:, own], weight_buf, in_sem.at[2]),
+        pltpu.make_async_copy(fwd_hbm, fwd_buf, in_sem.at[3]),
+        pltpu.make_async_copy(bwd_hbm, bwd_buf, in_sem.at[4]),
+        pltpu.make_async_copy(q_hbm, q_buf, in_sem.at[5]),
+    ]
+    for load in loads:
+        load.start()
+    loads[0].wait()
+    loads[1].wait()
+
+    @pl.loop(0, n)
+    def _(d):
+        for c in range(chunks):
+            at = pl.ds(pl.multiple_of(d * width + c * LANES, LANES), LANES)
+            product = k_buf[:, at].astype(jnp.float32) * v_buf[:, at].astype(jnp.float32)
+            mixed[c, d] = product.astype(jnp.bfloat16)
+
+    pl.semaphore_wait(barrier, n - 1 + m - 1)
+
+    def out_copy(c, k):
+        peer = seq_peer(k)
+        return pltpu.make_async_remote_copy(
+            src_ref=mixed.at[c, peer], dst_ref=data.at[c, me],
+            send_sem=send1.at[c, peer], recv_sem=recv1.at[c, me],
+            device_id=(peer, lane), device_id_type=MESH,
+        )
+
+    def in_copy(c, k):
+        peer = seq_peer(k)
+        return pltpu.make_async_remote_copy(
+            src_ref=mixed.at[c, peer], dst_ref=data.at[c, peer],
+            send_sem=send1.at[c, peer], recv_sem=recv1.at[c, peer],
+            device_id=(peer, lane), device_id_type=MESH,
+        )
+
+    def out_back(c, peer):
+        return pltpu.make_async_remote_copy(
+            src_ref=conv.at[c, peer], dst_ref=back.at[c, me],
+            send_sem=send2.at[c, peer], recv_sem=recv2.at[c, me],
+            device_id=(peer, lane), device_id_type=MESH,
+        )
+
+    def in_back(c, peer):
+        return pltpu.make_async_remote_copy(
+            src_ref=conv.at[c, peer], dst_ref=back.at[c, peer],
+            send_sem=send2.at[c, peer], recv_sem=recv2.at[c, peer],
+            device_id=(peer, lane), device_id_type=MESH,
+        )
+
+    for c in range(chunks):
+        for k in order:
+            out_copy(c, k).start()
+    for c in range(chunks):
+        data[c, me] = mixed[c, me]
+
+    hidden = jnp.tanh(jnp.dot(feats_ref[...], pos_ref[...], precision=HIGHEST, preferred_element_type=jnp.float32))
+    loads[2].wait()
+    rates = rates_ref[:, own]
+    gain = jnp.sqrt(2.0 * rates)
+    for i in range(n):
+        part = hidden[i * rows:(i + 1) * rows]
+        profile = jnp.dot(part, weight_buf[...], precision=HIGHEST, preferred_element_type=jnp.float32)
+        time = (lax.broadcasted_iota(jnp.int32, (rows, width), 0) + i * rows).astype(jnp.float32)
+        taps[pl.ds(i * rows, rows), :] = (jnp.exp(-rates * time) * gain * profile).astype(jnp.bfloat16)
+    loads[3].wait()
+
+    @pl.loop(0, length // block)
+    def _(b):
+        at = pl.ds(pl.multiple_of(b * 2 * block, 2 * block), 2 * block)
+        filt_spec[at, :] = jnp.dot(fwd_buf[at, :], taps[...], preferred_element_type=jnp.float32)
+
+    loads[4].wait()
+    for c in range(chunks):
+        for k in order:
+            in_copy(c, k).wait_recv()
+        held = data.at[c]
+
+        @pl.loop(0, length // block)
+        def _(b):
+            at = pl.ds(pl.multiple_of(b * 2 * block, 2 * block), 2 * block)
+            x = jnp.dot(fwd_buf[at, :], held[...].reshape(length, LANES), preferred_element_type=jnp.float32)
+            h = filt_spec[at, pl.ds(c * LANES, LANES)]
+            xc, xs, hc, hs = x[:block], x[block:], h[:block], h[block:]
+            both = jnp.concatenate([xc * hc - xs * hs, xc * hs + xs * hc], axis=0)
+            spec[at, :] = both.astype(jnp.bfloat16)
+
+        pairs = n // 2
+        for step in [(pairs // 2 + i) % pairs for i in range(pairs)]:
+            pair = lax.rem(me // 2 + step, pairs)
+            at = pl.ds(pl.multiple_of(pair * 2 * rows, 2 * rows), 2 * rows)
+            part = jnp.dot(bwd_buf[at, :], spec[...], preferred_element_type=jnp.float32)
+            conv[c, pl.ds(pair * 2, 2)] = part.astype(jnp.bfloat16).reshape(2, rows, LANES)
+            if step:
+                for half in range(2):
+                    out_back(c, pair * 2 + half).start()
+            else:
+                out_back(c, pair * 2 + 1 - lax.rem(me, 2)).start()
+        back[c, me] = conv[c, me]
+
+    loads[5].wait()
+    squares = jnp.zeros((rows, LANES), jnp.float32)
+    for c in range(chunks):
+        for k in [0] + order[::-1]:
+            peer = seq_peer(k)
+            if k:
+                in_back(c, peer).wait_recv()
+            at = pl.ds(pl.multiple_of(peer * width + c * LANES, LANES), LANES)
+            total = back[c, peer].astype(jnp.float32) + skip_ref[:, at] * mixed[c, peer].astype(jnp.float32)
+            gated = q_buf[:, at].astype(jnp.float32) * total
+            gated_ref[:, at] = gated
+            squares = squares + gated * gated
+    eye = lax.broadcasted_iota(jnp.int32, (rows, LANES), 0) == lax.broadcasted_iota(jnp.int32, (rows, LANES), 1)
+    column = jnp.sum(squares, axis=1, keepdims=True)
+    line = jnp.sum(jnp.where(eye, column, 0.0), axis=0, keepdims=True)
+    sums_out[...] = jnp.broadcast_to(line, sums_out.shape)
+
+    def sums_copy(k, mine):
+        peer = lax.rem(lane + k, m)
+        slot = lane if mine else peer
+        return pltpu.make_async_remote_copy(
+            src_ref=sums_out, dst_ref=sums_in.at[slot],
+            send_sem=send3.at[peer], recv_sem=recv3.at[slot],
+            device_id=(me, peer), device_id_type=MESH,
+        )
+
+    for k in range(1, m):
+        sums_copy(k, True).start()
+    total = sums_out[...]
+    for k in range(1, m):
+        sums_copy(k, False).wait_recv()
+        total = total + sums_in[lax.rem(lane + k, m)]
+    inv = lax.rsqrt(total[:1] / (cols * m) + 1e-06)
+    inv_ref[...] = jnp.sum(jnp.where(eye, inv, 0.0), axis=1, keepdims=True)
+
+    for c in range(chunks):
+        for k in order:
+            out_copy(c, k).wait_send()
+            out_back(c, seq_peer(k)).wait_send()
+    for k in range(1, m):
+        sums_copy(k, True).wait_send()
+
+
+def fused(queries, key_in, values, decay_rates, skip_gain, out_gain, pos_weight, filt_weight):
+    rows, cols = queries.shape
+    n, m = lax.axis_size("seq"), lax.axis_size("chan")
+    length, width = rows * n, cols // n
+    chunks = width // LANES
+    block = min(LANES, length)
+    forward, backward = (jnp.asarray(t) for t in spectral_tables(length, block))
+    vmem = pl.BlockSpec(memory_space=pltpu.VMEM)
+    hbm = pl.BlockSpec(memory_space=pl.ANY)
+    bf16, f32 = jnp.bfloat16, jnp.float32
+    dma = pltpu.SemaphoreType.DMA
+    gated, inv = pl.pallas_call(
+        functools.partial(kernel, n, m, block),
+        out_shape=(
+            jax.ShapeDtypeStruct((rows, cols), f32),
+            jax.ShapeDtypeStruct((rows, 1), f32),
+        ),
+        in_specs=[hbm, hbm, hbm, vmem, vmem, vmem, vmem, hbm, hbm, hbm],
+        out_specs=(vmem, vmem),
+        scratch_shapes=[
+            pltpu.VMEM((rows, cols), bf16),
+            pltpu.VMEM((rows, cols), bf16),
+            pltpu.VMEM((rows, cols), bf16),
+            pltpu.VMEM((filt_weight.shape[0], width), f32),
+            pltpu.VMEM((2 * length, length), bf16),
+            pltpu.VMEM((length, 2 * length), bf16),
+            pltpu.VMEM((chunks, n, rows, LANES), bf16),
+            pltpu.VMEM((chunks, n, rows, LANES), bf16),
+            pltpu.VMEM((length, width), bf16),
+            pltpu.VMEM((2 * length, width), f32),
+            pltpu.VMEM((2 * length, LANES), bf16),
+            pltpu.VMEM((chunks, n, rows, LANES), bf16),
+            pltpu.VMEM((chunks, n, rows, LANES), bf16),
+            pltpu.VMEM((8, LANES), f32),
+            pltpu.VMEM((m, 8, LANES), f32),
+            dma((6,)),
+            dma((chunks, n)),
+            dma((chunks, n)),
+            dma((chunks, n)),
+            dma((chunks, n)),
+            dma((m,)),
+            dma((m,)),
+        ],
+        compiler_params=pltpu.CompilerParams(
+            collective_id=0, has_side_effects=True, vmem_limit_bytes=40 * 1024 * 1024
+        ),
+    )(
+        queries, key_in, values, decay_rates[None, :], skip_gain[None, :],
+        jnp.asarray(feature_table(length)), pos_weight, filt_weight, forward, backward,
+    )
+    return gated * inv * out_gain[None, :]
+
+
+def local(queries, *others):
+    rows, cols = queries.shape
+    n = lax.axis_size("seq")
+    if rows == LANES and n % 4 == 0 and cols % (LANES * n) == 0:
+        return fused(queries, *others)
+    return plain(queries, *others)
+
+
 def solution(mesh):
     in_specs = (
         P("seq", "chan"),
@@ -70,5 +300,5 @@
         P(None, "chan"),
     )
     return jax.shard_map(
-        plain, mesh=mesh, in_specs=in_specs, out_specs=P("seq", "chan"), check_vma=False
+        local, mesh=mesh, in_specs=in_specs, out_specs=P("seq", "chan"), check_vma=False
     )

time: 60 us -> 49.7 us (0.83)
  Pallas kernels: 0 us -> 36.2 us
  waiting for transfers between devices: 21.5 us -> 0 us
  matrix products: 12.4 us -> 0 us
  starting transfers between devices: 11.1 us -> 0 us
  blocking collectives: 5.66 us -> 0 us
  local copies, waits for them, and re-layouts: 6.82 us -> 11.7 us
  other arithmetic: 1.97 us -> 1.23 us
    pallas_call x0 -> x1, Pallas kernels: none -> 36.2 us  [fused(): pl.pallas_call(functools.partial(kernel, n, m, block), out_shape=(jax.Sha...]
    all_to_all x2 -> x0, waiting for transfers between devices: 21.5 us -> none  [the longest x1 14.4 us: plain(): conv = lax.all_to_all(conv, 'seq', 0, 1, tiled=True).astype(jnp.float32)]
    dot_general x6 -> x0, matrix products: 12.4 us -> none  [the longest x1 4.79 us: plain(): filt_spec = jnp.dot(forward, taps, preferred_element_type=jnp.float32)]
    all_to_all x2 -> x0, starting transfers between devices: 11.1 us -> none  [the longest x1 7.28 us: plain(): data = lax.all_to_all(mixed, 'seq', 1, 0, tiled=True)]
    unnamed x21 -> x22, local copies, waits for them, and re-layouts: 3.61 us -> 11.7 us
    psum x1 -> x0, blocking collectives: 5.66 us -> none  [plain(): row_sums = lax.psum(jnp.sum(gated * gated, axis=1), 'chan')]
    all_to_all x2 -> x0, local copies, waits for them, and re-layouts: 1.9 us -> none  [the longest x1 1.01 us: plain(): data = lax.all_to_all(mixed, 'seq', 1, 0, tiled=True)]
    mul x1 -> x0, local copies, waits for them, and re-layouts: 1.31 us -> none  [plain(): return gated * inv_rms[:, None] * out_gain[None, :]]
  transfers between devices with their start and end apart: 2 -> 0, of which waited for: 2 -> 0; matrix products, arithmetic and copies ran while one was open for 13% -> 0% of each run, Pallas kernels for 0% -> 0%
where the time goes in v2:
time: 49.7 us; the launch traced here: 49.1 us
  Pallas kernels  36.2 us (73%)
  local copies, waits for them, and re-layouts  11.7 us (24%)
  other arithmetic  1.23 us (2%)
    pallas_call x1, Pallas kernels, fused(): pl.pallas_call(functools.partial(kernel, n, m, block), out_shape=(jax.Sha...  36.2 us
    unnamed x22, local copies, waits for them, and re-layouts  11.7 us
    mul x1, other arithmetic, fused(): return gated * inv * out_gain[None, :]  1.13 us

profile of v2, /device:TPU:0, one launch (start us, length us, event | category | flops | bytes accessed | tf_op | source)
XLA Modules:
  0.0 49.1 jit_solution(10446445757264344556)
XLA Ops:
  0.0 0.0 copy-start
  0.0 2.2 %copy-done = bf16[1024,2048]{1,0:T(8,128)(2,1)S(1)} copy-done((bf16[1024,2048]{1,0:T(8,128)(2,1)S(1)}, bf16[1024,2048]{1,0:T(8,128)(2,1)}, u32[]{:S(2)}) %copy-start) | copy-done | bytes 4194328
  2.2 0.0 copy-start.1
  2.2 2.2 %copy-done.1 = bf16[2048,1024]{1,0:T(8,128)(2,1)S(1)} copy-done((bf16[2048,1024]{1,0:T(8,128)(2,1)S(1)}, bf16[2048,1024]{1,0:T(8,128)(2,1)}, u32[]{:S(2)}) %copy-start.1) | copy-done | bytes 4194328
  4.4 0.0 copy-start.2
  4.4 1.0 %copy-done.2 = bf16[128,2048]{1,0:T(8,128)(2,1)S(1)} copy-done((bf16[128,2048]{1,0:T(8,128)(2,1)S(1)}, bf16[128,2048]{1,0:T(8,128)(2,1)}, u32[]{:S(2)}) %copy-start.2) | copy-done | bytes 524312
  5.4 0.0 copy-start.3
  5.4 1.0 %copy-done.3 = bf16[128,2048]{1,0:T(8,128)(2,1)S(1)} copy-done((bf16[128,2048]{1,0:T(8,128)(2,1)S(1)}, bf16[128,2048]{1,0:T(8,128)(2,1)}, u32[]{:S(2)}) %copy-start.3) | copy-done | bytes 524312
  6.5 0.0 copy-start.4
  6.5 1.0 %copy-done.4 = bf16[128,2048]{1,0:T(8,128)(2,1)S(1)} copy-done((bf16[128,2048]{1,0:T(8,128)(2,1)S(1)}, bf16[128,2048]{1,0:T(8,128)(2,1)}, u32[]{:S(2)}) %copy-start.4) | copy-done | bytes 524312
  7.5 0.0 copy-start.5
  7.5 1.0 %copy-done.5 = f32[64,2048]{1,0:T(8,128)S(1)} copy-done((f32[64,2048]{1,0:T(8,128)S(1)}, f32[64,2048]{1,0:T(8,128)}, u32[]{:S(2)}) %copy-start.5) | copy-done | bytes 524312
  8.5 0.0 copy-start.6
  8.5 1.0 %copy-done.6 = f32[1024,32]{1,0:T(8,128)S(1)} copy-done((f32[1024,32]{1,0:T(8,128)S(1)}, f32[1024,32]{1,0:T(8,128)}, u32[]{:S(2)}) %copy-start.6) | copy-done | bytes 131096
  9.6 0.0 copy-start.7
  9.6 0.7 %copy-done.7 = f32[32,64]{1,0:T(8,128)S(1)} copy-done((f32[32,64]{1,0:T(8,128)S(1)}, f32[32,64]{1,0:T(8,128)}, u32[]{:S(2)}) %copy-start.7) | copy-done | bytes 8216
  10.3 0.0 copy-start.8
  10.3 0.7 %copy-done.8 = f32[2048]{0:T(1024)S(1)} copy-done((f32[2048]{0:T(1024)S(1)}, f32[2048]{0:T(1024)}, u32[]{:S(2)}) %copy-start.8) | copy-done | bytes 8216
  11.0 0.0 copy-start.9
  11.0 0.7 %copy-done.9 = f32[2048]{0:T(1024)S(1)} copy-done((f32[2048]{0:T(1024)S(1)}, f32[2048]{0:T(1024)}, u32[]{:S(2)}) %copy-start.9) | copy-done | bytes 8216
  11.7 0.0 copy-start.10
  11.7 36.2 %shard_map.109 = (f32[128,2048]{1,0:T(8,128)S(1)}, f32[128,1]{1,0:T(8,128)S(1)}) custom-call(bf16[128,2048]{1,0:T(8,128)(2,1)S(1)} %copy-done.2, bf16[128,2048]{1,0:T(8,128)(2,1)S(1)} %copy-done.3, bf16[128,2048]{1,0:T(8,128)(2,1)S(1)} %copy-done.4, f32[1,2048]{1,0:T(1,128)S(1)} %bitcast.2, f32[1,2048]{1,0:T(1,128)S(1)} %bitcast.3, ...), custom_call_target="tpu_custom_call" | custom-call | tf_op jit(solution)/shard_map/pallas_call | solution.py:241
  47.9 0.1 reduce
  48.0 0.0 copy-done.10
  48.0 1.1 %multiply_multiply_fusion = f32[128,2048]{1,0:T(8,128)} fusion(f32[128,2048]{1,0:T(8,128)S(1)} %get-tuple-element.7, f32[2048]{0:T(1024)S(1)} %copy-done.10, f32[128]{0:T(128)S(1)} %reduce), kind=kLoop, calls=%fused_computation | loop fusion | flops 524288 | bytes 2105856 | tf_op jit(solution)/shard_map/mul | solution.py:280
Async XLA Ops:
  0.0 2.2 %copy-start = (bf16[1024,2048]{1,0:T(8,128)(2,1)S(1)}, bf16[1024,2048]{1,0:T(8,128)(2,1)}, u32[]{:S(2)}) copy-start(bf16[1024,2048]{1,0:T(8,128)(2,1)} %constant.7.clone.bwd_hbm) | copy-start | bytes 12582916
  2.2 2.2 %copy-start.1 = (bf16[2048,1024]{1,0:T(8,128)(2,1)S(1)}, bf16[2048,1024]{1,0:T(8,128)(2,1)}, u32[]{:S(2)}) copy-start(bf16[2048,1024]{1,0:T(8,128)(2,1)} %constant.6.clone.fwd_hbm) | copy-start | bytes 12582916
  4.4 1.0 %copy-start.2 = (bf16[128,2048]{1,0:T(8,128)(2,1)S(1)}, bf16[128,2048]{1,0:T(8,128)(2,1)}, u32[]{:S(2)}) copy-start(bf16[128,2048]{1,0:T(8,128)(2,1)} %q_hbm.1) | copy-start | bytes 1572868
  5.4 1.0 %copy-start.3 = (bf16[128,2048]{1,0:T(8,128)(2,1)S(1)}, bf16[128,2048]{1,0:T(8,128)(2,1)}, u32[]{:S(2)}) copy-start(bf16[128,2048]{1,0:T(8,128)(2,1)} %k_hbm.1) | copy-start | bytes 1572868
  6.5 1.0 %copy-start.4 = (bf16[128,2048]{1,0:T(8,128)(2,1)S(1)}, bf16[128,2048]{1,0:T(8,128)(2,1)}, u32[]{:S(2)}) copy-start(bf16[128,2048]{1,0:T(8,128)(2,1)} %v_hbm.1) | copy-start | bytes 1572868
  7.5 1.0 %copy-start.5 = (f32[64,2048]{1,0:T(8,128)S(1)}, f32[64,2048]{1,0:T(8,128)}, u32[]{:S(2)}) copy-start(f32[64,2048]{1,0:T(8,128)} %weight_hbm.1) | copy-start | bytes 1572868
  8.5 1.0 %copy-start.6 = (f32[1024,32]{1,0:T(8,128)S(1)}, f32[1024,32]{1,0:T(8,128)}, u32[]{:S(2)}) copy-start(f32[1024,32]{1,0:T(8,128)} %constant.8.clone.feats_ref) | copy-start | bytes 393220
  9.6 0.7 %copy-start.7 = (f32[32,64]{1,0:T(8,128)S(1)}, f32[32,64]{1,0:T(8,128)}, u32[]{:S(2)}) copy-start(f32[32,64]{1,0:T(8,128)} %pos_ref.1) | copy-start | bytes 24580
  10.3 0.7 %copy-start.8 = (f32[2048]{0:T(1024)S(1)}, f32[2048]{0:T(1024)}, u32[]{:S(2)}) copy-start(f32[2048]{0:T(1024)} %param.14) | copy-start | bytes 24580
  11.0 0.7 %copy-start.9 = (f32[2048]{0:T(1024)S(1)}, f32[2048]{0:T(1024)}, u32[]{:S(2)}) copy-start(f32[2048]{0:T(1024)} %param.15) | copy-start | bytes 24580
  11.7 36.3 %copy-start.10 = (f32[2048]{0:T(1024)S(1)}, f32[2048]{0:T(1024)}, u32[]{:S(2)}) copy-start(f32[2048]{0:T(1024)} %param.16) | copy-start | bytes 24580

commit v3 on v2

--- a/solution.py
+++ b/solution.py
@@ -60,11 +60,11 @@
 
 def kernel(
     n, m, block,
-    q_hbm, k_hbm, v_hbm, rates_ref, skip_ref, feats_ref, pos_ref, weight_hbm, fwd_hbm, bwd_hbm,
-    gated_ref, inv_ref,
-    q_buf, k_buf, v_buf, weight_buf, fwd_buf, bwd_buf,
+    q_hbm, k_hbm, v_hbm, rates_hbm, skip_hbm, gain_hbm, feats_hbm, pos_hbm, weight_hbm, fwd_hbm, bwd_hbm,
+    out_hbm,
+    q_buf, k_buf, v_buf, rates_ref, skip_ref, gain_ref, feats_ref, pos_ref, weight_buf, fwd_buf, bwd_buf,
     mixed, data, taps, filt_spec, spec, conv, back, sums_out, sums_in,
-    in_sem, send1, recv1, send2, recv2, send3, recv3,
+    gated_ref, in_sem, key_sem, value_sem, out_sem, send1, recv1, send2, recv2, send3, recv3,
 ):
     rows, cols = q_buf.shape
     length, width = taps.shape
@@ -82,26 +82,42 @@
         pl.semaphore_signal(barrier, inc=1, device_id=(me, lax.rem(lane + k, m)), device_id_type=MESH)
 
     own = pl.ds(pl.multiple_of(me * width, LANES), width)
+    def piece(k):
+        return pl.ds(pl.multiple_of(seq_peer(k) * width, LANES), width)
+
+    pieces = order + [0]
+    firsts = [
+        (
+            pltpu.make_async_copy(k_hbm.at[:, piece(k)], k_buf.at[:, piece(k)], key_sem.at[k]),
+            pltpu.make_async_copy(v_hbm.at[:, piece(k)], v_buf.at[:, piece(k)], value_sem.at[k]),
+        )
+        for k in pieces
+    ]
+    for pair in firsts:
+        for load in pair:
+            load.start()
     loads = [
-        pltpu.make_async_copy(k_hbm, k_buf, in_sem.at[0]),
-        pltpu.make_async_copy(v_hbm, v_buf, in_sem.at[1]),
-        pltpu.make_async_copy(weight_hbm.at[:, own], weight_buf, in_sem.at[2]),
-        pltpu.make_async_copy(fwd_hbm, fwd_buf, in_sem.at[3]),
-        pltpu.make_async_copy(bwd_hbm, bwd_buf, in_sem.at[4]),
-        pltpu.make_async_copy(q_hbm, q_buf, in_sem.at[5]),
+        pltpu.make_async_copy(feats_hbm, feats_ref, in_sem.at[0]),
+        pltpu.make_async_copy(pos_hbm, pos_ref, in_sem.at[1]),
+        pltpu.make_async_copy(rates_hbm.at[:, own], rates_ref, in_sem.at[2]),
+        pltpu.make_async_copy(weight_hbm.at[:, own], weight_buf, in_sem.at[3]),
+        pltpu.make_async_copy(fwd_hbm, fwd_buf, in_sem.at[4]),
+        pltpu.make_async_copy(bwd_hbm, bwd_buf, in_sem.at[5]),
+        pltpu.make_async_copy(skip_hbm, skip_ref, in_sem.at[6]),
+        pltpu.make_async_copy(q_hbm, q_buf, in_sem.at[7]),
+        pltpu.make_async_copy(gain_hbm, gain_ref, in_sem.at[8]),
     ]
-    for load in loads:
-        load.start()
-    loads[0].wait()
-    loads[1].wait()
-
-    @pl.loop(0, n)
-    def _(d):
+
+    def mix(i):
+        for load in firsts[i]:
+            load.wait()
+        d = seq_peer(pieces[i])
         for c in range(chunks):
             at = pl.ds(pl.multiple_of(d * width + c * LANES, LANES), LANES)
             product = k_buf[:, at].astype(jnp.float32) * v_buf[:, at].astype(jnp.float32)
             mixed[c, d] = product.astype(jnp.bfloat16)
 
+    mix(0)
     pl.semaphore_wait(barrier, n - 1 + m - 1)
 
     def out_copy(c, k):
@@ -134,29 +150,39 @@
             device_id=(peer, lane), device_id_type=MESH,
         )
 
-    for c in range(chunks):
+    for i, k in enumerate(order):
+        if i:
+            mix(i)
+        out_copy(0, k).start()
+    for c in range(1, chunks):
         for k in order:
             out_copy(c, k).start()
+    for load in loads:
+        load.start()
+    mix(n - 1)
     for c in range(chunks):
         data[c, me] = mixed[c, me]
 
+    loads[0].wait()
+    loads[1].wait()
     hidden = jnp.tanh(jnp.dot(feats_ref[...], pos_ref[...], precision=HIGHEST, preferred_element_type=jnp.float32))
     loads[2].wait()
-    rates = rates_ref[:, own]
+    loads[3].wait()
+    rates = rates_ref[...]
     gain = jnp.sqrt(2.0 * rates)
     for i in range(n):
         part = hidden[i * rows:(i + 1) * rows]
         profile = jnp.dot(part, weight_buf[...], precision=HIGHEST, preferred_element_type=jnp.float32)
         time = (lax.broadcasted_iota(jnp.int32, (rows, width), 0) + i * rows).astype(jnp.float32)
         taps[pl.ds(i * rows, rows), :] = (jnp.exp(-rates * time) * gain * profile).astype(jnp.bfloat16)
-    loads[3].wait()
+    loads[4].wait()
 
     @pl.loop(0, length // block)
     def _(b):
         at = pl.ds(pl.multiple_of(b * 2 * block, 2 * block), 2 * block)
         filt_spec[at, :] = jnp.dot(fwd_buf[at, :], taps[...], preferred_element_type=jnp.float32)
 
-    loads[4].wait()
+    loads[5].wait()
     for c in range(chunks):
         for k in order:
             in_copy(c, k).wait_recv()
@@ -184,7 +210,8 @@
                 out_back(c, pair * 2 + 1 - lax.rem(me, 2)).start()
         back[c, me] = conv[c, me]
 
-    loads[5].wait()
+    loads[6].wait()
+    loads[7].wait()
     squares = jnp.zeros((rows, LANES), jnp.float32)
     for c in range(chunks):
         for k in [0] + order[::-1]:
@@ -217,7 +244,14 @@
         sums_copy(k, False).wait_recv()
         total = total + sums_in[lax.rem(lane + k, m)]
     inv = lax.rsqrt(total[:1] / (cols * m) + 1e-06)
-    inv_ref[...] = jnp.sum(jnp.where(eye, inv, 0.0), axis=1, keepdims=True)
+    inv = jnp.sum(jnp.where(eye, inv, 0.0), axis=1, keepdims=True)
+    loads[8].wait()
+    stores = []
+    for d in range(n):
+        at = pl.ds(d * width, width)
+        gated_ref[:, at] = gated_ref[:, at] * inv * gain_ref[:, at]
+        stores.append(pltpu.make_async_copy(gated_ref.at[:, at], out_hbm.at[:, at], out_sem.at[d]))
+        stores[-1].start()
 
     for c in range(chunks):
         for k in order:
@@ -225,6 +259,8 @@
             out_back(c, seq_peer(k)).wait_send()
     for k in range(1, m):
         sums_copy(k, True).wait_send()
+    for store in stores:
+        store.wait()
 
 
 def fused(queries, key_in, values, decay_rates, skip_gain, out_gain, pos_weight, filt_weight):
@@ -232,24 +268,25 @@
     n, m = lax.axis_size("seq"), lax.axis_size("chan")
     length, width = rows * n, cols // n
     chunks = width // LANES
-    block = min(LANES, length)
+    block = min(2 * LANES, length)
     forward, backward = (jnp.asarray(t) for t in spectral_tables(length, block))
-    vmem = pl.BlockSpec(memory_space=pltpu.VMEM)
-    hbm = pl.BlockSpec(memory_space=pl.ANY)
+    hbm = pl.BlockSpec(memory_space=pltpu.HBM)
     bf16, f32 = jnp.bfloat16, jnp.float32
     dma = pltpu.SemaphoreType.DMA
-    gated, inv = pl.pallas_call(
+    return pl.pallas_call(
         functools.partial(kernel, n, m, block),
-        out_shape=(
-            jax.ShapeDtypeStruct((rows, cols), f32),
-            jax.ShapeDtypeStruct((rows, 1), f32),
-        ),
-        in_specs=[hbm, hbm, hbm, vmem, vmem, vmem, vmem, hbm, hbm, hbm],
-        out_specs=(vmem, vmem),
+        out_shape=jax.ShapeDtypeStruct((rows, cols), f32),
+        in_specs=[hbm] * 11,
+        out_specs=hbm,
         scratch_shapes=[
             pltpu.VMEM((rows, cols), bf16),
             pltpu.VMEM((rows, cols), bf16),
             pltpu.VMEM((rows, cols), bf16),
+            pltpu.VMEM((1, width), f32),
+            pltpu.VMEM((1, cols), f32),
+            pltpu.VMEM((1, cols), f32),
+            pltpu.VMEM((length, 2 * FREQS), f32),
+            pltpu.VMEM(pos_weight.shape, f32),
             pltpu.VMEM((filt_weight.shape[0], width), f32),
             pltpu.VMEM((2 * length, length), bf16),
             pltpu.VMEM((length, 2 * length), bf16),
@@ -262,7 +299,11 @@
             pltpu.VMEM((chunks, n, rows, LANES), bf16),
             pltpu.VMEM((8, LANES), f32),
             pltpu.VMEM((m, 8, LANES), f32),
-            dma((6,)),
+            pltpu.VMEM((rows, cols), f32),
+            dma((9,)),
+            dma((n,)),
+            dma((n,)),
+            dma((n,)),
             dma((chunks, n)),
             dma((chunks, n)),
             dma((chunks, n)),
@@ -271,13 +312,12 @@
             dma((m,)),
         ],
         compiler_params=pltpu.CompilerParams(
-            collective_id=0, has_side_effects=True, vmem_limit_bytes=40 * 1024 * 1024
+            collective_id=0, has_side_effects=True, vmem_limit_bytes=63 * 1024 * 1024
         ),
     )(
-        queries, key_in, values, decay_rates[None, :], skip_gain[None, :],
+        queries, key_in, values, decay_rates[None, :], skip_gain[None, :], out_gain[None, :],
         jnp.asarray(feature_table(length)), pos_weight, filt_weight, forward, backward,
     )
-    return gated * inv * out_gain[None, :]
 
 
 def local(queries, *others):

time: 49.7 us -> 37.9 us (0.76)
  local copies, waits for them, and re-layouts: 11.7 us -> 2.3 us
  other arithmetic: 1.23 us -> 0 us
  Pallas kernels: 36.2 us -> 35.4 us
    unnamed x22 -> x1, local copies, waits for them, and re-layouts: 11.7 us -> 2.3 us
    mul x1 -> x0, other arithmetic: 1.13 us -> none  [fused(): return gated * inv * out_gain[None, :]]
    pallas_call x1, Pallas kernels: 36.2 us -> 35.4 us  [fused(): pl.pallas_call(functools.partial(kernel, n, m, block), out_shape=jax.Shap...]
where the time goes in v3:
time: 37.9 us; the launch traced here: 37.7 us
  Pallas kernels  35.4 us (93%)
  local copies, waits for them, and re-layouts  2.3 us (6%)
    pallas_call x1, Pallas kernels, fused(): pl.pallas_call(functools.partial(kernel, n, m, block), out_shape=jax.Shap...  35.4 us
    unnamed x1, local copies, waits for them, and re-layouts  2.3 us

profile of v3, /device:TPU:0, one launch (start us, length us, event | category | flops | bytes accessed | tf_op | source)
XLA Modules:
  0.0 37.7 jit_solution(6940444671149693651)
XLA Ops:
  0.0 35.4 %shard_map.109 = f32[128,2048]{1,0:T(8,128)} custom-call(bf16[128,2048]{1,0:T(8,128)(2,1)} %q_hbm.1, bf16[128,2048]{1,0:T(8,128)(2,1)} %k_hbm.1, bf16[128,2048]{1,0:T(8,128)(2,1)} %v_hbm.1, f32[1,2048]{1,0:T(1,128)} %bitcast.3, f32[1,2048]{1,0:T(1,128)} %bitcast.4, f32[1,2048]{1,0:T(1,128)} %bitcast.5, f32[1024,32]{1,0:T(8,128)} %constant.8.clone.feats_hbm, ...), custom_call_target="tpu_custom_call" | custom-call | tf_op jit(solution)/shard_map/pallas_call | solution.py:276
  35.4 2.3 %copy.13 = f32[128,2048]{1,0:T(8,128)} copy(f32[128,2048]{1,0:T(8,128)} %shard_map.109) | data formatting | bytes 2097152
